TPU v7x, 32 devices: a whole 2x2x4 slice. The times are simulated.
32 devices in a mesh: event: 4 (over z), blk: 8 (over y, x, core).
Axes of the slice: x: 2, y: 2, z: 4, core: 2. Of those that a mesh axis runs over, the one named last changes fastest.
Arguments:
- features: bfloat16 [4, 192, 64, 512], P('event', 'blk'), may hold values from -6 to 6
- occupancy: int32 [4, 192, 512], P('event', 'blk'), may hold values 0 or 1
- block_cells: int32 [4, 192], P('event'), may hold values from 0 to 63, as said below
- weight: bfloat16 [27, 64, 64], replicated, may hold values from -0.15625 to 0.15625
- cotangent: bfloat16 [4, 192, 64, 512], P('event', 'blk'), may hold values from -6 to 6
Outputs:
- output: bfloat16 [4, 192, 64, 512], P('event', 'blk')
- grad_features: bfloat16 [4, 192, 64, 512], P('event', 'blk')
- grad_weight: float32 [27, 64, 64], replicated
Inputs may be any that keep to these rules, and one draw needn't show every extreme that they name: `block_cells`: blocks of an event are listed plane by plane, 24 to a plane, planes 0 to 7 in order; within a plane the cells are distinct and increasing. Index i of blk owns plane i.
All inputs are finite; a program needn't handle non-finite values. No bound on the sum of `occupancy` on one device may be relied on, other than what follows from the above.
Results may differ from a plain program's by a relative error of at most 0.001.
Values may be sent and summed in bfloat16 or wider, within the bound.
A program may use at most 128 MiB of HBM per device.

v0:
```python
import math
import jax
import jax.numpy as jnp
from jax import lax
from jax.sharding import PartitionSpec as P

CHANNELS = 64
EDGE = 8
VOXELS = 512
TAPS = 27
GRID_Y = 8
GRID_Z = 8
CELLS = 64
ACTIVE = 24


def shifted(x, axis, by):
    devices = lax.axis_size(axis)
    pairs = [(i, i + by) for i in range(devices) if 0 <= i + by < devices]
    return lax.ppermute(x, axis, pairs)


def offset_list():
    return [
        (step_x, step_y, step_z)
        for step_x in (-1, 0, 1)
        for step_y in (-1, 0, 1)
        for step_z in (-1, 0, 1)
    ]


def ranges_for(offset_step):
    if offset_step < 0:
        return (slice(0, 1), slice(EDGE - 1, EDGE))
    if offset_step > 0:
        return (slice(EDGE + 1, EDGE + 2), slice(0, 1))
    return (slice(1, EDGE + 1), slice(0, EDGE))


def neighbour_slots(own_plane, own_cells, table_gid, offset):
    row_y = own_cells // GRID_Z + offset[1]
    row_z = own_cells % GRID_Z + offset[2]
    inside = (row_y >= 0) & (row_y < GRID_Y) & (row_z >= 0) & (row_z < GRID_Z)
    target = (own_plane + offset[0]) * CELLS + row_y * GRID_Z + row_z
    matches = (target[:, None] == table_gid[None, :]) & inside[:, None]
    present = jnp.any(matches, axis=1)
    listing = jnp.arange(table_gid.shape[0], dtype=jnp.int32)[None, :]
    position = jnp.sum(jnp.where(matches, listing, 0), axis=1)
    return (present, position)


def build_padded(centre, table, own_plane, own_cells, table_gid):
    count = centre.shape[0]
    padded = jnp.zeros((count, CHANNELS, EDGE + 2, EDGE + 2, EDGE + 2), centre.dtype)
    padded = padded.at[:, :, 1 : EDGE + 1, 1 : EDGE + 1, 1 : EDGE + 1].set(centre)
    for offset in offset_list():
        if offset == (0, 0, 0):
            continue
        present, position = neighbour_slots(own_plane, own_cells, table_gid, offset)
        dest_x, source_x = ranges_for(offset[0])
        dest_y, source_y = ranges_for(offset[1])
        dest_z, source_z = ranges_for(offset[2])
        slab = table[:, :, source_x, source_y, source_z]
        picked = jnp.take(slab, position, axis=0)
        picked = jnp.where(present[:, None, None, None, None], picked, jnp.zeros_like(picked))
        padded = padded.at[:, :, dest_x, dest_y, dest_z].set(picked)
    return padded


def columns(padded, orient):
    pieces = []
    for offset in offset_list():
        starts = [1 + orient * offset_step for offset_step in offset]
        piece = padded[
            :,
            :,
            starts[0] : starts[0] + EDGE,
            starts[1] : starts[1] + EDGE,
            starts[2] : starts[2] + EDGE,
        ]
        pieces.append(piece.reshape(padded.shape[0], CHANNELS, VOXELS))
    return jnp.concatenate(pieces, axis=1)


def extended(local, below_face, above_face):
    empty = jnp.zeros((ACTIVE, CHANNELS, EDGE, EDGE, EDGE), jnp.bfloat16)
    below_block = empty.at[:, :, EDGE - 1].set(below_face.reshape(ACTIVE, CHANNELS, EDGE, EDGE))
    above_block = empty.at[:, :, 0].set(above_face.reshape(ACTIVE, CHANNELS, EDGE, EDGE))
    return jnp.concatenate([below_block, local, above_block], axis=0)


def per_device(features, occupancy, block_cells, weight, cotangent):
    device = lax.axis_index("blk")
    count = features.shape[1]
    plane_count = count // ACTIVE
    face_size = CHANNELS * EDGE * EDGE
    mask_half = occupancy[0].astype(jnp.bfloat16)
    masked = features[0] * mask_half[:, None, :]
    grad_masked = cotangent[0] * mask_half[:, None, :]
    volume = masked.reshape(count, CHANNELS, EDGE, EDGE, EDGE)
    grad_volume = grad_masked.reshape(count, CHANNELS, EDGE, EDGE, EDGE)
    paired = jnp.stack([volume, grad_volume])
    low_faces = paired[:, :ACTIVE, :, 0].reshape(2, ACTIVE, face_size)
    high_faces = paired[:, count - ACTIVE :, :, EDGE - 1].reshape(2, ACTIVE, face_size)
    from_below = shifted(high_faces, "blk", 1)
    from_above = shifted(low_faces, "blk", -1)
    filler = jnp.full((ACTIVE,), -1, jnp.int32)
    padded_cells = jnp.concatenate([filler, block_cells[0], filler])
    cells_ext = lax.dynamic_slice_in_dim(padded_cells, device * count, (plane_count + 2) * ACTIVE)
    ext_plane = jnp.arange((plane_count + 2) * ACTIVE, dtype=jnp.int32) // ACTIVE
    table_gid = jnp.where(cells_ext >= 0, ext_plane * CELLS + cells_ext, -5)
    own_cells = cells_ext[ACTIVE : ACTIVE + count]
    own_plane = jnp.arange(count, dtype=jnp.int32) // ACTIVE + 1
    table_x = extended(volume, from_below[0], from_above[0])
    table_g = extended(grad_volume, from_below[1], from_above[1])
    padded = build_padded(volume, table_x, own_plane, own_cells, table_gid)
    grad_padded = build_padded(grad_volume, table_g, own_plane, own_cells, table_gid)
    w_flat = weight.reshape(TAPS * CHANNELS, CHANNELS)
    w_back = jnp.transpose(weight, (1, 0, 2)).reshape(CHANNELS, TAPS * CHANNELS)
    group = math.gcd(count, 4)
    group_count = count // group
    shape_p = (group_count, group, CHANNELS, EDGE + 2, EDGE + 2, EDGE + 2)
    mask_full = occupancy[0].astype(jnp.float32).reshape(group_count, group, VOXELS)

    def group_terms(inner):
        padded_p, grad_padded_p, mask_p, grad_masked_p = inner
        col_x = columns(padded_p, 1)
        col_g = columns(grad_padded_p, -1)
        result = jnp.einsum("kc,bkv->bcv", w_flat, col_x, preferred_element_type=jnp.float32)
        out_p = (result * mask_p[:, None, :]).astype(jnp.bfloat16)
        grad_w = jnp.einsum("bkv,bcv->kc", col_x, grad_masked_p, preferred_element_type=jnp.float32)
        back = jnp.einsum("ik,bkv->biv", w_back, col_g, preferred_element_type=jnp.float32)
        grad_p = (back * mask_p[:, None, :]).astype(jnp.bfloat16)
        return (out_p, grad_p, grad_w)

    outs_p, grads_p, weights_p = lax.map(
        group_terms,
        (
            padded.reshape(shape_p),
            grad_padded.reshape(shape_p),
            mask_full,
            grad_masked.reshape(group_count, group, CHANNELS, VOXELS),
        ),
    )
    local_grad = jnp.sum(weights_p, axis=0)
    grad_weight = lax.psum(local_grad, ("event", "blk"))
    grad_weight = grad_weight.reshape(TAPS, CHANNELS, CHANNELS)
    output = outs_p.reshape(count, CHANNELS, VOXELS)[None]
    grad_features = grads_p.reshape(count, CHANNELS, VOXELS)[None]
    return (output, grad_features, grad_weight)


def solution(mesh):
    in_specs = (
        P("event", "blk", None, None),
        P("event", "blk", None),
        P("event", None),
        P(),
        P("event", "blk", None, None),
    )
    out_specs = (P("event", "blk", None, None), P("event", "blk", None, None), P())
    return jax.shard_map(
        per_device, mesh=mesh, in_specs=in_specs, out_specs=out_specs, check_vma=False
    )
```

profile of v0, /device:TPU:0, one launch (start us, length us, event | category | flops | bytes accessed | tf_op | source)
XLA Modules:
  0.0 1134.5 jit_solution(11747880840834999203)
XLA Ops:
  9.0 4.1 copy.831
  15.9 4.3 broadcast_multiply_fusion.1
  21.4 4.2 copy.834
  31.5 5.4 copy.838
  60.3 4.3 broadcast_multiply_fusion.2
  116.5 6.7 fusion.17
  287.7 699.8 %while.72 = (s32[]{:T(128)}, bf16[6,4,64,512]{3,2,1,0:T(8,128)(2,1)}, bf16[6,4,64,512]{3,2,1,0:T(8,128)(2,1)}, f32[6,1728,64]{1,2,0:T(8,128)}, bf16[6,4,64,10,10...) while((s32[]{:T(128)}, ...), condition=%wide.region_53.61_spmd, body=%wide.region_52.60_spmd.sunk | while | flops 1359478784 | bytes 151677424 | solution.py:136
  307.4 4.0 fusion.204
  342.3 5.2 fusion.205
  396.3 6.2 fusion.206
  424.0 4.0 fusion.204
  458.9 5.2 fusion.205
  512.9 6.1 fusion.206
  540.6 4.0 fusion.204
  575.5 5.2 fusion.205
  629.5 6.1 fusion.206
  657.2 4.0 fusion.204
  692.1 5.2 fusion.205
  746.1 6.1 fusion.206
  808.7 5.2 fusion.205
  862.7 6.2 fusion.206
  925.3 5.2 fusion.205
  979.4 6.2 fusion.206
  991.0 133.9 %all-reduce.8.cloned.1.call-done = f32[27,64,64]{1,0,2:T(8,128)} async-done(((f32[27,64,64]{1,0,2:T(8,128)}), f32[27,64,64]{1,0,2:T(8,128)}) %all-reduce.8.cloned.1.call-update) | async-done | bytes 442384 | tf_op jit(solution)/shard_map/psum | solution.py:146
  (1159 shorter events, 869.2 us)
Async XLA Ops:
  7.2 1117.7 %all-reduce.8.cloned.1.call-start = ((), (), s32[]{:S(2)}) async-start(), calls=%async_computation | async-start | bytes 2097152 | tf_op jit(solution)/shard_map/psum | solution.py:146
  21.4 19.5 %copy-start.54 = (s32[1,192]{1,0:T(1,128)S(1)}, s32[1,192]{1,0:T(1,128)}, u32[]{:S(2)}) copy-start(s32[1,192]{1,0:T(1,128)} %param.139) | copy-start | bytes 2308
  25.7 19.2 %copy-start.14 = (bf16[1,24,64,512]{3,2,1,0:T(8,128)(2,1)S(1)}, bf16[1,24,64,512]{3,2,1,0:T(8,128)(2,1)}, u32[]{:S(2)}) copy-start(bf16[1,24,64,512]{3,2,1,0:T(8,128)(2,1)} %param.137) | copy-start | bytes 4718596
  28.3 65.4 %collective-permute-start = (bf16[2,24,4096]{2,1,0:T(8,128)(2,1)}, bf16[2,24,4096]{2,1,0:T(8,128)(2,1)}, u32[]{:S(2)}, u32[]{:S(2)}) collective-permute-start(bf16[2,24,4096]{2,1,0:T(8,128)(2,1)} %copy.835), channel_id=1, source_target_pairs={{0,1},{1,2},{2,3},{3,4},{4,5},{5,6},{6,7},{8,9},{9,10},{10,11},{11... | collective-permute-start | bytes 1179656 | tf_op jit(solution)/shard_map/ppermute | solution.py:20
  39.4 59.7 %collective-permute-start.1 = (bf16[2,24,4096]{2,1,0:T(8,128)(2,1)}, bf16[2,24,4096]{2,1,0:T(8,128)(2,1)}, u32[]{:S(2)}, u32[]{:S(2)}) collective-permute-start(bf16[2,24,4096]{2,1,0:T(8,128)(2,1)} %copy.839), channel_id=1, source_target_pairs={{1,0},{2,1},{3,2},{4,3},{5,4},{6,5},{7,6},{9,8},{10,9},{11,10},{12... | collective-permute-start | bytes 1179656 | tf_op jit(solution)/shard_map/ppermute | solution.py:20
  91.0 151.1 %copy-start.53 = (s32[1024]{0:T(1024)}, s32[1024]{0:T(1024)S(1)}, u32[]{:S(2)}) copy-start(s32[1024]{0:T(1024)S(1)} %pad_clamp_fusion) | copy-start | bytes 12292
  244.8 24.9 %copy-start.24 = (bf16[24,64,8]{1,2,0:T(8,128)(2,1)S(1)}, bf16[24,64,8]{1,2,0:T(8,128)(2,1)}, u32[]{:S(2)}) copy-start(bf16[24,64,8]{1,2,0:T(8,128)(2,1)} %gather_fusion.14) | copy-start | bytes 73732
  244.9 24.9 %copy-start.25 = (bf16[24,64,8]{1,2,0:T(8,128)(2,1)S(1)}, bf16[24,64,8]{1,2,0:T(8,128)(2,1)}, u32[]{:S(2)}) copy-start(bf16[24,64,8]{1,2,0:T(8,128)(2,1)} %gather_fusion.40) | copy-start | bytes 73732
  244.9 28.4 %copy-start.26 = (bf16[24,64,8]{1,2,0:T(8,128)(2,1)S(1)}, bf16[24,64,8]{1,2,0:T(8,128)(2,1)}, u32[]{:S(2)}) copy-start(bf16[24,64,8]{1,2,0:T(8,128)(2,1)} %gather_fusion.16) | copy-start | bytes 73732
  244.9 28.4 %copy-start.27 = (bf16[24,64,8]{1,2,0:T(8,128)(2,1)S(1)}, bf16[24,64,8]{1,2,0:T(8,128)(2,1)}, u32[]{:S(2)}) copy-start(bf16[24,64,8]{1,2,0:T(8,128)(2,1)} %gather_fusion.42) | copy-start | bytes 73732
  244.9 29.9 %copy-start.51 = (bf16[24,64]{1,0:T(8,128)(2,1)S(1)}, bf16[24,64]{1,0:T(8,128)(2,1)}, u32[]{:S(2)}) copy-start(bf16[24,64]{1,0:T(8,128)(2,1)} %gather_fusion.17) | copy-start | bytes 9220
  244.9 29.9 %copy-start.52 = (bf16[24,64]{1,0:T(8,128)(2,1)S(1)}, bf16[24,64]{1,0:T(8,128)(2,1)}, u32[]{:S(2)}) copy-start(bf16[24,64]{1,0:T(8,128)(2,1)} %gather_fusion.43) | copy-start | bytes 9220
  244.9 31.2 %copy-start.22 = (bf16[24,64,8]{1,2,0:T(8,128)(2,1)S(1)}, bf16[24,64,8]{1,2,0:T(8,128)(2,1)}, u32[]{:S(2)}) copy-start(bf16[24,64,8]{1,2,0:T(8,128)(2,1)} %gather_fusion.18) | copy-start | bytes 73732
  244.9 31.2 %copy-start.23 = (bf16[24,64,8]{1,2,0:T(8,128)(2,1)S(1)}, bf16[24,64,8]{1,2,0:T(8,128)(2,1)}, u32[]{:S(2)}) copy-start(bf16[24,64,8]{1,2,0:T(8,128)(2,1)} %gather_fusion.44) | copy-start | bytes 73732
  244.9 32.6 %copy-start.49 = (bf16[24,64]{1,0:T(8,128)(2,1)S(1)}, bf16[24,64]{1,0:T(8,128)(2,1)}, u32[]{:S(2)}) copy-start(bf16[24,64]{1,0:T(8,128)(2,1)} %gather_fusion.19) | copy-start | bytes 9220
  244.9 32.6 %copy-start.50 = (bf16[24,64]{1,0:T(8,128)(2,1)S(1)}, bf16[24,64]{1,0:T(8,128)(2,1)}, u32[]{:S(2)}) copy-start(bf16[24,64]{1,0:T(8,128)(2,1)} %gather_fusion.45) | copy-start | bytes 9220
  244.9 33.9 %copy-start.18 = (bf16[24,64,8]{1,2,0:T(8,128)(2,1)S(1)}, bf16[24,64,8]{1,2,0:T(8,128)(2,1)}, u32[]{:S(2)}) copy-start(bf16[24,64,8]{1,2,0:T(8,128)(2,1)} %gather_fusion.20) | copy-start | bytes 73732
  245.0 33.9 %copy-start.19 = (bf16[24,64,8]{1,2,0:T(8,128)(2,1)S(1)}, bf16[24,64,8]{1,2,0:T(8,128)(2,1)}, u32[]{:S(2)}) copy-start(bf16[24,64,8]{1,2,0:T(8,128)(2,1)} %gather_fusion.46) | copy-start | bytes 73732
  245.0 37.4 %copy-start.20 = (bf16[24,64,8]{1,2,0:T(8,128)(2,1)S(1)}, bf16[24,64,8]{1,2,0:T(8,128)(2,1)}, u32[]{:S(2)}) copy-start(bf16[24,64,8]{1,2,0:T(8,128)(2,1)} %gather_fusion.48) | copy-start | bytes 73732
  245.0 37.4 %copy-start.21 = (bf16[24,64,8]{1,2,0:T(8,128)(2,1)S(1)}, bf16[24,64,8]{1,2,0:T(8,128)(2,1)}, u32[]{:S(2)}) copy-start(bf16[24,64,8]{1,2,0:T(8,128)(2,1)} %gather_fusion.22) | copy-start | bytes 73732
  245.0 38.8 %copy-start.47 = (bf16[24,64]{1,0:T(8,128)(2,1)S(1)}, bf16[24,64]{1,0:T(8,128)(2,1)}, u32[]{:S(2)}) copy-start(bf16[24,64]{1,0:T(8,128)(2,1)} %gather_fusion.49) | copy-start | bytes 9220
  245.0 38.7 %copy-start.48 = (bf16[24,64]{1,0:T(8,128)(2,1)S(1)}, bf16[24,64]{1,0:T(8,128)(2,1)}, u32[]{:S(2)}) copy-start(bf16[24,64]{1,0:T(8,128)(2,1)} %gather_fusion.23) | copy-start | bytes 9220
  245.0 40.1 %copy-start.16 = (bf16[24,64,8]{1,2,0:T(8,128)(2,1)S(1)}, bf16[24,64,8]{1,2,0:T(8,128)(2,1)}, u32[]{:S(2)}) copy-start(bf16[24,64,8]{1,2,0:T(8,128)(2,1)} %gather_fusion.50) | copy-start | bytes 73732
  245.0 40.1 %copy-start.17 = (bf16[24,64,8]{1,2,0:T(8,128)(2,1)S(1)}, bf16[24,64,8]{1,2,0:T(8,128)(2,1)}, u32[]{:S(2)}) copy-start(bf16[24,64,8]{1,2,0:T(8,128)(2,1)} %gather_fusion.24) | copy-start | bytes 73732
  (94 other events, 1105.8 us)
Sparse Core Ops, SparseCore 0:
  991.1 133.7 all-reduce.7
where the time goes:
time: 1150 us; the launch traced here: 1130 us
  local copies, waits for them, and re-layouts  808 us (70%)
  waiting for transfers between devices  134 us (12%)
  other arithmetic  89.4 us (8%)
  matrix products  80.3 us (7%)
  between operations  15 us (1%)
    reshape x324, local copies, waits for them, and re-layouts, columns(): pieces.append(piece.reshape(padded.shape[0], CHANNELS, VOXELS))  287 us
    while x456, local copies, waits for them, and re-layouts  226 us
    psum x1, waiting for transfers between devices, per_device(): grad_weight = lax.psum(local_grad, ('event', 'blk'))  134 us
    gather x52, local copies, waits for them, and re-layouts, build_padded(): picked = jnp.take(slab, position, axis=0)  76.1 us
    slice x24, local copies, waits for them, and re-layouts, columns(): padded[:, :, starts[0]:starts[0] + EDGE, starts[1]:starts[1] + EDGE, star...  73.4 us
    another operation x50, local copies, waits for them, and re-layouts, build_padded(): picked = jnp.take(slab, position, axis=0)  44.9 us
    scatter x26, other arithmetic, build_padded(): padded = padded.at[:, :, dest_x, dest_y, dest_z].set(picked)  42.7 us
    dot_general x6, matrix products, group_terms(): jnp.einsum('bkv,bcv->kc', col_x, grad_masked_p, preferred_element_type=jn...  36.9 us
  transfers between devices with their start and end apart: 3, of which 1 were waited for; matrix products, arithmetic and copies ran while one was open for 6% of the time, Pallas kernels for 0%

commit v1 on v0

--- a/solution.py
+++ b/solution.py
@@ -143,7 +143,7 @@
         ),
     )
     local_grad = jnp.sum(weights_p, axis=0)
-    grad_weight = lax.psum(local_grad, ("event", "blk"))
+    grad_weight = lax.psum(lax.psum(local_grad, "blk"), "event")
     grad_weight = grad_weight.reshape(TAPS, CHANNELS, CHANNELS)
     output = outs_p.reshape(count, CHANNELS, VOXELS)[None]
     grad_features = grads_p.reshape(count, CHANNELS, VOXELS)[None]

time: 1150 us -> 1130 us (0.983)
  waiting for transfers between devices: 134 us -> 110 us
    psum x1 -> x2, waiting for transfers between devices: 134 us -> 110 us  [per_device(): grad_weight = lax.psum(lax.psum(local_grad, 'blk'), 'event')]
  transfers between devices with their start and end apart: 3 -> 4, of which waited for: 1 -> 2; matrix products, arithmetic and copies ran while one was open for 6% -> 6% of each run, Pallas kernels for 0% -> 0%
where the time goes in v1:
time: 1130 us; the launch traced here: 1110 us
  local copies, waits for them, and re-layouts  809 us (72%)
  waiting for transfers between devices  110 us (10%)
  other arithmetic  90.2 us (8%)
  matrix products  80.3 us (7%)
  between operations  15 us (1%)
    reshape x324, local copies, waits for them, and re-layouts, columns(): pieces.append(piece.reshape(padded.shape[0], CHANNELS, VOXELS))  287 us
    while x456, local copies, waits for them, and re-layouts  226 us
    psum x2, waiting for transfers between devices, per_device(): grad_weight = lax.psum(lax.psum(local_grad, 'blk'), 'event')  110 us
    gather x52, local copies, waits for them, and re-layouts, build_padded(): picked = jnp.take(slab, position, axis=0)  76.1 us
    slice x24, local copies, waits for them, and re-layouts, columns(): padded[:, :, starts[0]:starts[0] + EDGE, starts[1]:starts[1] + EDGE, star...  73.4 us
    another operation x50, local copies, waits for them, and re-layouts, build_padded(): picked = jnp.take(slab, position, axis=0)  44.9 us
    scatter x26, other arithmetic, build_padded(): padded = padded.at[:, :, dest_x, dest_y, dest_z].set(picked)  42.7 us
    dot_general x6, matrix products, group_terms(): jnp.einsum('bkv,bcv->kc', col_x, grad_masked_p, preferred_element_type=jn...  36.9 us
  transfers between devices with their start and end apart: 4, of which 2 were waited for; matrix products, arithmetic and copies ran while one was open for 6% of the time, Pallas kernels for 0%

profile of v1, /device:TPU:0, one launch (start us, length us, event | category | flops | bytes accessed | tf_op | source)
XLA Modules:
  0.0 1112.1 jit_solution(5228855871583383305)
XLA Ops:
  9.0 4.1 copy.831
  15.9 4.3 broadcast_multiply_fusion.1
  21.4 4.2 copy.834
  31.5 5.4 copy.838
  60.3 4.3 broadcast_multiply_fusion.2
  116.5 6.7 fusion.17
  287.7 699.8 %while.72 = (s32[]{:T(128)}, bf16[6,4,64,512]{3,2,1,0:T(8,128)(2,1)}, bf16[6,4,64,512]{3,2,1,0:T(8,128)(2,1)}, f32[6,1728,64]{1,2,0:T(8,128)}, bf16[6,4,64,10,10...) while((s32[]{:T(128)}, ...), condition=%wide.region_53.61_spmd, body=%wide.region_52.60_spmd.sunk | while | flops 1359478784 | bytes 151677424 | solution.py:136
  307.4 4.0 fusion.204
  342.3 5.2 fusion.205
  396.3 6.2 fusion.206
  424.0 4.0 fusion.204
  458.9 5.2 fusion.205
  512.9 6.1 fusion.206
  540.6 4.0 fusion.204
  575.5 5.2 fusion.205
  629.5 6.1 fusion.206
  692.1 5.2 fusion.205
  746.1 6.1 fusion.206
  808.7 5.2 fusion.205
  862.7 6.2 fusion.206
  925.3 5.2 fusion.205
  979.4 6.2 fusion.206
  990.4 58.4 %all-reduce.9.cloned.1.call-done = f32[1728,64]{0,1:T(8,128)} async-done(((f32[1728,64]{0,1:T(8,128)}), f32[1728,64]{0,1:T(8,128)}) %all-reduce.9.cloned.1.call-update) | async-done | bytes 442384 | tf_op jit(solution)/shard_map/psum | solution.py:146
  1051.2 51.3 %all-reduce.11.cloned.1.call-done = f32[27,64,64]{1,0,2:T(8,128)} async-done(((f32[27,64,64]{1,0,2:T(8,128)}), f32[27,64,64]{1,0,2:T(8,128)}) %all-reduce.11.cloned.1.call-update) | async-done | bytes 442384 | tf_op jit(solution)/shard_map/psum | solution.py:146
  (1162 shorter events, 875.0 us)
Async XLA Ops:
  7.2 1041.5 %all-reduce.9.cloned.1.call-start = ((), (), s32[]{:S(2)}) async-start(), calls=%async_computation | async-start | bytes 917504 | tf_op jit(solution)/shard_map/psum | solution.py:146
  21.4 19.5 %copy-start.54 = (s32[1,192]{1,0:T(1,128)S(1)}, s32[1,192]{1,0:T(1,128)}, u32[]{:S(2)}) copy-start(s32[1,192]{1,0:T(1,128)} %param.139) | copy-start | bytes 2308
  28.3 65.4 %collective-permute-start = (bf16[2,24,4096]{2,1,0:T(8,128)(2,1)}, bf16[2,24,4096]{2,1,0:T(8,128)(2,1)}, u32[]{:S(2)}, u32[]{:S(2)}) collective-permute-start(bf16[2,24,4096]{2,1,0:T(8,128)(2,1)} %copy.835), channel_id=1, source_target_pairs={{0,1},{1,2},{2,3},{3,4},{4,5},{5,6},{6,7},{8,9},{9,10},{10,11},{11... | collective-permute-start | bytes 1179656 | tf_op jit(solution)/shard_map/ppermute | solution.py:20
  39.4 59.7 %collective-permute-start.1 = (bf16[2,24,4096]{2,1,0:T(8,128)(2,1)}, bf16[2,24,4096]{2,1,0:T(8,128)(2,1)}, u32[]{:S(2)}, u32[]{:S(2)}) collective-permute-start(bf16[2,24,4096]{2,1,0:T(8,128)(2,1)} %copy.839), channel_id=1, source_target_pairs={{1,0},{2,1},{3,2},{4,3},{5,4},{6,5},{7,6},{9,8},{10,9},{11,10},{12... | collective-permute-start | bytes 1179656 | tf_op jit(solution)/shard_map/ppermute | solution.py:20
  91.0 151.1 %copy-start.53 = (s32[1024]{0:T(1024)}, s32[1024]{0:T(1024)S(1)}, u32[]{:S(2)}) copy-start(s32[1024]{0:T(1024)S(1)} %pad_clamp_fusion) | copy-start | bytes 12292
  244.8 24.9 %copy-start.24 = (bf16[24,64,8]{1,2,0:T(8,128)(2,1)S(1)}, bf16[24,64,8]{1,2,0:T(8,128)(2,1)}, u32[]{:S(2)}) copy-start(bf16[24,64,8]{1,2,0:T(8,128)(2,1)} %gather_fusion.14) | copy-start | bytes 73732
  244.9 24.9 %copy-start.25 = (bf16[24,64,8]{1,2,0:T(8,128)(2,1)S(1)}, bf16[24,64,8]{1,2,0:T(8,128)(2,1)}, u32[]{:S(2)}) copy-start(bf16[24,64,8]{1,2,0:T(8,128)(2,1)} %gather_fusion.40) | copy-start | bytes 73732
  244.9 28.4 %copy-start.26 = (bf16[24,64,8]{1,2,0:T(8,128)(2,1)S(1)}, bf16[24,64,8]{1,2,0:T(8,128)(2,1)}, u32[]{:S(2)}) copy-start(bf16[24,64,8]{1,2,0:T(8,128)(2,1)} %gather_fusion.16) | copy-start | bytes 73732
  244.9 28.4 %copy-start.27 = (bf16[24,64,8]{1,2,0:T(8,128)(2,1)S(1)}, bf16[24,64,8]{1,2,0:T(8,128)(2,1)}, u32[]{:S(2)}) copy-start(bf16[24,64,8]{1,2,0:T(8,128)(2,1)} %gather_fusion.42) | copy-start | bytes 73732
  244.9 29.9 %copy-start.51 = (bf16[24,64]{1,0:T(8,128)(2,1)S(1)}, bf16[24,64]{1,0:T(8,128)(2,1)}, u32[]{:S(2)}) copy-start(bf16[24,64]{1,0:T(8,128)(2,1)} %gather_fusion.17) | copy-start | bytes 9220
  244.9 29.9 %copy-start.52 = (bf16[24,64]{1,0:T(8,128)(2,1)S(1)}, bf16[24,64]{1,0:T(8,128)(2,1)}, u32[]{:S(2)}) copy-start(bf16[24,64]{1,0:T(8,128)(2,1)} %gather_fusion.43) | copy-start | bytes 9220
  244.9 31.2 %copy-start.22 = (bf16[24,64,8]{1,2,0:T(8,128)(2,1)S(1)}, bf16[24,64,8]{1,2,0:T(8,128)(2,1)}, u32[]{:S(2)}) copy-start(bf16[24,64,8]{1,2,0:T(8,128)(2,1)} %gather_fusion.18) | copy-start | bytes 73732
  244.9 31.2 %copy-start.23 = (bf16[24,64,8]{1,2,0:T(8,128)(2,1)S(1)}, bf16[24,64,8]{1,2,0:T(8,128)(2,1)}, u32[]{:S(2)}) copy-start(bf16[24,64,8]{1,2,0:T(8,128)(2,1)} %gather_fusion.44) | copy-start | bytes 73732
  244.9 32.6 %copy-start.49 = (bf16[24,64]{1,0:T(8,128)(2,1)S(1)}, bf16[24,64]{1,0:T(8,128)(2,1)}, u32[]{:S(2)}) copy-start(bf16[24,64]{1,0:T(8,128)(2,1)} %gather_fusion.19) | copy-start | bytes 9220
  244.9 32.6 %copy-start.50 = (bf16[24,64]{1,0:T(8,128)(2,1)S(1)}, bf16[24,64]{1,0:T(8,128)(2,1)}, u32[]{:S(2)}) copy-start(bf16[24,64]{1,0:T(8,128)(2,1)} %gather_fusion.45) | copy-start | bytes 9220
  244.9 33.9 %copy-start.18 = (bf16[24,64,8]{1,2,0:T(8,128)(2,1)S(1)}, bf16[24,64,8]{1,2,0:T(8,128)(2,1)}, u32[]{:S(2)}) copy-start(bf16[24,64,8]{1,2,0:T(8,128)(2,1)} %gather_fusion.20) | copy-start | bytes 73732
  245.0 33.9 %copy-start.19 = (bf16[24,64,8]{1,2,0:T(8,128)(2,1)S(1)}, bf16[24,64,8]{1,2,0:T(8,128)(2,1)}, u32[]{:S(2)}) copy-start(bf16[24,64,8]{1,2,0:T(8,128)(2,1)} %gather_fusion.46) | copy-start | bytes 73732
  245.0 37.4 %copy-start.20 = (bf16[24,64,8]{1,2,0:T(8,128)(2,1)S(1)}, bf16[24,64,8]{1,2,0:T(8,128)(2,1)}, u32[]{:S(2)}) copy-start(bf16[24,64,8]{1,2,0:T(8,128)(2,1)} %gather_fusion.48) | copy-start | bytes 73732
  245.0 37.4 %copy-start.21 = (bf16[24,64,8]{1,2,0:T(8,128)(2,1)S(1)}, bf16[24,64,8]{1,2,0:T(8,128)(2,1)}, u32[]{:S(2)}) copy-start(bf16[24,64,8]{1,2,0:T(8,128)(2,1)} %gather_fusion.22) | copy-start | bytes 73732
  245.0 38.8 %copy-start.47 = (bf16[24,64]{1,0:T(8,128)(2,1)S(1)}, bf16[24,64]{1,0:T(8,128)(2,1)}, u32[]{:S(2)}) copy-start(bf16[24,64]{1,0:T(8,128)(2,1)} %gather_fusion.49) | copy-start | bytes 9220
  245.0 38.7 %copy-start.48 = (bf16[24,64]{1,0:T(8,128)(2,1)S(1)}, bf16[24,64]{1,0:T(8,128)(2,1)}, u32[]{:S(2)}) copy-start(bf16[24,64]{1,0:T(8,128)(2,1)} %gather_fusion.23) | copy-start | bytes 9220
  245.0 40.1 %copy-start.16 = (bf16[24,64,8]{1,2,0:T(8,128)(2,1)S(1)}, bf16[24,64,8]{1,2,0:T(8,128)(2,1)}, u32[]{:S(2)}) copy-start(bf16[24,64,8]{1,2,0:T(8,128)(2,1)} %gather_fusion.50) | copy-start | bytes 73732
  245.0 40.1 %copy-start.17 = (bf16[24,64,8]{1,2,0:T(8,128)(2,1)S(1)}, bf16[24,64,8]{1,2,0:T(8,128)(2,1)}, u32[]{:S(2)}) copy-start(bf16[24,64,8]{1,2,0:T(8,128)(2,1)} %gather_fusion.24) | copy-start | bytes 73732
  990.3 112.1 %all-reduce.11.cloned.1.call-start = ((), (), s32[]{:S(2)}) async-start(), calls=%async_computation.1 | async-start | bytes 2097152 | tf_op jit(solution)/shard_map/psum | solution.py:146
  (95 other events, 1125.0 us)
Sparse Core Ops, SparseCore 0:
  990.4 58.2 all-reduce.8
  1051.3 51.1 all-reduce.10
